TPU v7x, 128 devices: a whole 4x4x4 slice. The times are simulated.
128 devices in a mesh: patch: 128 (over x, z, y, core).
Axes of the slice: x: 4, y: 4, z: 4, core: 2. Of those that a mesh axis runs over, the one named last changes fastest.
Arguments:
- noisy: float32 [1024, 4, 4, 1024], P('patch'), may hold values from -12 to 12
- sigma: float32 [4], replicated, may hold values from 0.5 to 4
- coarse: bfloat16 [12, 131072], P(None, 'patch'), may hold values from -6 to 6
- row_ids: int32 [1024, 16], P('patch'), may hold values from 0 to 131071, as said below
- table_index: int32 [1024], P('patch'), may hold values from 0 to 7
- interp_table: bfloat16 [8, 16, 1024], replicated, may hold values from -1.5 to 1.5
- live_counts: int32 [128], P('patch'), may hold values from 1 to 4
- face_len: int32 [1024, 2], P('patch'), may hold values from 1 to 32
- w_lift: bfloat16 [128, 16], replicated, may hold values from -1.5 to 1.5
- noise_embed: float32 [128], replicated, may hold values from -6 to 6
- kernel_top: bfloat16 [9, 128, 128], replicated, may hold values from -0.1875 to 0.1875
- w_down: bfloat16 [256, 128], replicated, may hold values from -0.5 to 0.5
- kernel_mid: bfloat16 [9, 256, 256], replicated, may hold values from -0.125 to 0.125
- w_up: bfloat16 [128, 256], replicated, may hold values from -0.375 to 0.375
- kernel_dec: bfloat16 [9, 128, 128], replicated, may hold values from -0.1875 to 0.1875
- w_out: bfloat16 [4, 128], replicated, may hold values from -0.5 to 0.5
Outputs:
- stepped: float32 [1024, 4, 4, 1024], P('patch')
Inputs may be any that keep to these rules, and one draw needn't show every extreme that they name: `row_ids`: the coarse cells of patch p are local: each lies in [b * 1024 - 1024/2, (b + 1) * 1024 + 1024/2) with b = p // 8, the block of coarse cells held with the patch widened by half a block on each side.
All inputs are finite; a program needn't handle non-finite values.
Results may differ from a plain program's by a relative error of at most 0.00053.
Values may be sent and summed in bfloat16 or wider, within the bound.
A program may use at most 384 MiB of HBM per device.

v0:
```python
import functools

import jax
import jax.numpy as jnp
from jax import lax
from jax.experimental import pallas as pl
from jax.experimental.pallas import tpu as pltpu
from jax.sharding import PartitionSpec as P

MESH = pl.DeviceIdType.MESH
bf16 = jnp.bfloat16
f32 = jnp.float32

SLOTS = 8
ENS = 4
C = 128
C2 = 256
ROWS = 512
MROWS = 256
SIGMA_DATA = 0.5
STEP_RATIO = 0.25
EPSILON = 1e-06

NT = (((1,), (1,)), ((), ()))


def iota(shape, dim):
    return lax.broadcasted_iota(jnp.int32, shape, dim)


def half_silu(v, scale):
    h = v * scale
    return h + h * jnp.tanh(h)


def act_pair(v):
    halves = []
    for k in range(2):
        x = v[:, k * C : (k + 1) * C]
        scale = 0.5 * lax.rsqrt(jnp.mean(x * x, axis=1, keepdims=True) + EPSILON)
        halves.append(half_silu(x, scale))
    return halves


def act_wide(v):
    scale = 0.5 * lax.rsqrt(jnp.mean(v * v, axis=1, keepdims=True) + EPSILON)
    return half_silu(v, scale)


def from_left(x):
    n, c = x.shape
    x3 = x.reshape(n // 16, 16, c)
    return jnp.where(iota(x3.shape, 1) == 0, 0.0, pltpu.roll(x3, 1, 1)).reshape(n, c)


def from_right(x):
    n, c = x.shape
    x3 = x.reshape(n // 16, 16, c)
    return jnp.where(iota(x3.shape, 1) == 15, 0.0, pltpu.roll(x3, 15, 1)).reshape(n, c)


def transposed(block):
    return block.astype(f32).T.astype(bf16)


def kernel(
    noisy, sigma, coarse, row_ids, table_index, interp, live, face_len, w_lift, embed,
    k_top, w_down, k_mid, w_up, k_dec, w_out,
    out,
    cx, wtop, wdec, wmid, wup, wout, wlift, d_in,
    top, fc, fs, ha, hb, sha, shb, pool, mc, ml, mr, mha, mhb,
    rxa1, rxb1, rxa2, rxb2, rxa3, rxb3, send, recv,
):
    n = lax.axis_size("patch")
    me = lax.axis_index("patch")
    right, left = lax.rem(me + 1, n), lax.rem(me + n - 1, n)
    has_above = jnp.where(me > 0, 1.0, 0.0).astype(f32)
    has_below = jnp.where(me < n - 1, 1.0, 0.0).astype(f32)

    barrier = pltpu.get_barrier_semaphore()
    for neighbour in (left, right):
        pl.semaphore_signal(barrier, inc=1, device_id=(neighbour,), device_id_type=MESH)

    own = jnp.concatenate([coarse[...].astype(f32), jnp.zeros((4, 1024), f32)], axis=0)
    cx[:, 512:1536] = own.astype(bf16)

    pl.semaphore_wait(barrier, 2)

    def remote(src, dst, k, device):
        return pltpu.make_async_remote_copy(
            src_ref=src, dst_ref=dst, send_sem=send.at[k], recv_sem=recv.at[k],
            device_id=(device,), device_id_type=MESH,
        )

    cells_right = remote(cx.at[:, 1024:1536], cx.at[:, 0:512], 0, right)
    cells_left = remote(cx.at[:, 512:1024], cx.at[:, 1536:2048], 1, left)
    cells_right.start()
    cells_left.start()

    zero = jnp.zeros((C, C), bf16)
    for k_ref, w in ((k_top, wtop), (k_dec, wdec)):

        def fine_weights(dy, carry, k_ref=k_ref, w=w):
            taps = [transposed(k_ref[3 * dy + dx]) for dx in range(3)]
            rows = [(taps[1], taps[0]), (taps[2], taps[1]), (taps[0], zero), (zero, taps[2])]
            for i, (even, odd) in enumerate(rows):
                at = pl.multiple_of(dy * 512 + i * C, C)
                w[pl.ds(at, C), 0:C] = even
                w[pl.ds(at, C), C:C2] = odd
            return carry

        lax.fori_loop(0, 3, fine_weights, 0)

    def mid_weights(t, carry):
        wmid[pl.ds(pl.multiple_of(t * C2, C2), C2), :] = transposed(k_mid[t])
        return carry

    lax.fori_loop(0, 9, mid_weights, 0)
    wmid[2304:, :] = transposed(w_down[...])
    wup[...] = transposed(w_up[...])
    lane = iota((C, C), 0)
    for e in range(ENS):
        for par in range(2):
            z = jnp.zeros((C, C), f32)
            for v in range(4):
                row = w_out[v : v + 1, :].astype(f32)
                z = z + jnp.where(lane == par * 16 + e * 4 + v, row, 0.0)
            wout[e * C2 + par * C : e * C2 + (par + 1) * C, :] = z.T.astype(bf16)
        j = iota((C, 16), 0) % 32
        idx = iota((C, 16), 1)
        pick = ((j // 4 == e) & (idx == j % 4)) | ((j >= 16) & (j < 28) & (idx == j - 12))
        block = lax.dot_general(
            jnp.where(pick, 1.0, 0.0).astype(bf16), w_lift[...], NT, preferred_element_type=f32
        ).astype(bf16)
        wlift[e, 0:C, 0:C] = block
        wlift[e, 0:C, C:C2] = zero
        wlift[e, C:C2, 0:C] = zero
        wlift[e, C:C2, C:C2] = block

    def member(e, f):
        s = jnp.full((1, C), sigma[e], f32)
        return f(s)

    bias = []
    for e in range(ENS):
        b = embed[...] * member(e, jnp.log)
        bias.append(jnp.concatenate([b, b], axis=1))

    def per_row(f):
        r = iota((16, C), 0) // 4
        s = jnp.full((16, C), sigma[0], f32)
        for e in range(1, ENS):
            s = jnp.where(r == e, sigma[e], s)
        return f(s)[:, 0:1]

    c_in = per_row(lambda s: lax.rsqrt(s * s + SIGMA_DATA * SIGMA_DATA))
    c_skip = per_row(lambda s: SIGMA_DATA * SIGMA_DATA / (s * s + SIGMA_DATA * SIGMA_DATA))
    c_out = per_row(lambda s: s * SIGMA_DATA * lax.rsqrt(s * s + SIGMA_DATA * SIGMA_DATA))

    ids = row_ids[...] - (me * 1024 - 512)
    ids = jnp.concatenate([ids] * 8, axis=1)
    ids = jnp.where(iota((8, C), 1) // 16 == iota((8, C), 0), ids, 0)
    ids = jnp.sum(ids.astype(f32), axis=0, keepdims=True).astype(jnp.int32)
    one_hot = jnp.where(iota((2048, C), 0) == ids, 1.0, 0.0).astype(bf16)
    tab = jnp.zeros((C, C), jnp.int32)
    pk = iota((C, C), 0)
    tk = iota((C, C), 1)
    for p in range(SLOTS):
        tab = jnp.where(pk // 16 == p, table_index[p], tab)
    route = jnp.where((pk % 16 == tk % 16) & (tk // 16 == tab), 1.0, 0.0).astype(bf16)

    cells_right.wait()
    cells_left.wait()
    picked = jnp.dot(cx[...], one_hot, preferred_element_type=f32)
    picked = jnp.concatenate([picked] * 8, axis=0)
    picked = jnp.where(pk // 16 == tk // 16, picked, 0.0).astype(bf16)
    stencil = jnp.dot(picked, route, preferred_element_type=f32).astype(bf16)
    tables = interp[...].reshape(C, 1024)
    cond = jnp.dot(stencil, tables, preferred_element_type=f32).astype(bf16)
    for p in range(SLOTS):
        state = (noisy[p].reshape(16, 1024) * c_in).astype(bf16)
        for b in range(4):
            at = slice(b * C2, (b + 1) * C2)
            mr[b, p * 32 : p * 32 + 16, :] = state[:, at]
            mr[b, p * 32 + 16 : p * 32 + 32, :] = cond[p * 16 : p * 16 + 16, at]

    r = iota((C2, C2), 0)
    cell = iota((C2, C2), 1)
    split = jnp.where(cell == 2 * (r % C) + r // C, 1.0, 0.0).astype(bf16)
    for b in range(4):
        d = lax.dot_general(split, mr[b], NT, preferred_element_type=f32).astype(bf16)
        for t in range(2):
            for par in range(2):
                d_in[t, b * C : (b + 1) * C, par * C : (par + 1) * C] = d[
                    par * C : (par + 1) * C, t * C : (t + 1) * C
                ]

    fine_col = 2 * iota((16, C), 0)
    mid_col = 2 * iota((16, C2), 0)

    def alive(p):
        return jnp.where(jnp.minimum(p, SLOTS - 1 - p) < live[0], 1.0, 0.0).astype(f32)

    def face_of_next(p):
        return jnp.where(p == SLOTS - 1, 32, face_len[jnp.minimum(p + 1, SLOTS - 1), 0])

    def face_of_previous(p):
        return jnp.where(p == 0, 32, face_len[jnp.maximum(p - 1, 0), 1])

    def put_fine_face(centre, side, slot, e, even, odd, length, keep):
        even = jnp.where(fine_col < length, even, 0.0) * keep
        odd = jnp.where(fine_col + 1 < length, odd, 0.0) * keep
        centre[slot, e, :, 0:C] = even.astype(bf16)
        centre[slot, e, :, C:C2] = odd.astype(bf16)
        side[slot, e, :, 0:C] = from_left(odd).astype(bf16)
        side[slot, e, :, C:C2] = from_right(even).astype(bf16)

    def put_fine(p, e, even, odd):
        u = p * ENS + e
        fc[u, :, 0:C] = even.astype(bf16)
        fc[u, :, C:C2] = odd.astype(bf16)
        fs[u, :, 0:C] = from_left(odd).astype(bf16)
        fs[u, :, C:C2] = from_right(even).astype(bf16)
        keep = alive(p)
        put_fine_face(ha, sha, p + 1, e, even[ROWS - 16 :], odd[ROWS - 16 :], face_of_next(p), keep)
        put_fine_face(hb, shb, p, e, even[:16], odd[:16], face_of_previous(p), keep)

    def put_mid_face(faces, slot, e, a, length, keep):
        a = jnp.where(mid_col < length, a, 0.0) * keep
        faces[0, slot, e] = from_left(a).astype(bf16)
        faces[1, slot, e] = a.astype(bf16)
        faces[2, slot, e] = from_right(a).astype(bf16)

    def put_mid(p, e, a):
        u = p * ENS + e
        mc[u] = a.astype(bf16)
        ml[u] = from_left(a).astype(bf16)
        mr[u] = from_right(a).astype(bf16)
        keep = alive(p)
        put_mid_face(mha, p + 1, e, a[MROWS - 16 :], face_of_next(p), keep)
        put_mid_face(mhb, p, e, a[:16], face_of_previous(p), keep)

    def windows(ref, u, above, below, rows):
        return [
            jnp.concatenate([above, ref[u, 0 : rows - 16]], axis=0),
            ref[u],
            jnp.concatenate([ref[u, 16:rows], below], axis=0),
        ]

    def fine_conv(p, e, w):
        u = p * ENS + e
        centre = windows(fc, u, ha[p, e], hb[p + 1, e], ROWS)
        side = windows(fs, u, sha[p, e], shb[p + 1, e], ROWS)
        lhs = jnp.concatenate([x for pair in zip(centre, side) for x in pair], axis=1)
        return jnp.dot(lhs, w[...], preferred_element_type=f32)

    def mid_conv(p, e):
        u = p * ENS + e
        sides = [
            windows(ref, u, mha[k, p, e], mhb[k, p + 1, e], MROWS)
            for k, ref in enumerate((ml, mc, mr))
        ]
        taps = [sides[dx][dy] for dy in range(3) for dx in range(3)]
        lhs = jnp.concatenate(taps + [pool[u]], axis=1)
        return jnp.dot(lhs, wmid[...], preferred_element_type=f32)

    def fine_arrived(rxa, rxb):
        for e in range(ENS):
            a = rxa[e].astype(f32)
            put_fine_face(ha, sha, 0, e, a[:, :C], a[:, C:], face_len[0, 0], has_above)
            b = rxb[e].astype(f32)
            put_fine_face(hb, shb, SLOTS, e, b[:, :C], b[:, C:], face_len[SLOTS - 1, 1], has_below)

    def mid_arrived(rxa, rxb):
        for e in range(ENS):
            put_mid_face(mha, 0, e, rxa[e].astype(f32), face_len[0, 0], has_above)
            put_mid_face(mhb, SLOTS, e, rxb[e].astype(f32), face_len[SLOTS - 1, 1], has_below)

    def lift(i, carry):
        p = (i + 2) % SLOTS
        lanes = (iota((1, C2), 1) % C) // 32 == p % 4
        lhs = d_in[p // 4] * jnp.where(lanes, 1.0, 0.0).astype(bf16)
        for e in range(ENS):
            hidden = jnp.dot(lhs, wlift[e], preferred_element_type=f32) + bias[e]
            top[p * ENS + e] = hidden
            put_fine(p, e, *act_pair(hidden))
        return carry

    lax.fori_loop(0, SLOTS, lift, 0)
    face_down = remote(ha.at[SLOTS], rxa1, 2, right)
    face_up = remote(hb.at[0], rxb1, 3, left)
    face_down.start()
    face_up.start()

    def encode(i, carry):
        p = (i + 2) % SLOTS

        @pl.when(i == 5)
        def _():
            face_down.wait()
            face_up.wait()
            fine_arrived(rxa1, rxb1)

        for e in range(ENS):
            u = p * ENS + e
            t = top[u] + fine_conv(p, e, wtop)
            top[u] = t
            pooled = (t[:, :C] + t[:, C:]).reshape(16, 2, 16, C)
            pooled = ((pooled[:, 0] + pooled[:, 1]) * 0.25).reshape(MROWS, C).astype(bf16)
            pool[u] = pooled
            d = jnp.dot(pooled, wmid[2304:, :], preferred_element_type=f32)
            put_mid(p, e, act_wide(d))
        return carry

    lax.fori_loop(0, SLOTS, encode, 0)
    mid_down = remote(mha.at[1, SLOTS], rxa2, 4, right)
    mid_up = remote(mhb.at[1, 0], rxb2, 5, left)
    mid_down.start()
    mid_up.start()

    def middle(i, carry):
        p = (i + 2) % SLOTS

        @pl.when(i == 5)
        def _():
            mid_down.wait()
            mid_up.wait()
            mid_arrived(rxa2, rxb2)

        for e in range(ENS):
            u = p * ENS + e
            m = mid_conv(p, e).astype(bf16)
            up = jnp.dot(m, wup[...], preferred_element_type=f32).reshape(16, 1, 16, C)
            up = jnp.broadcast_to(up, (16, 2, 16, C)).reshape(ROWS, C)
            merged = top[u] + jnp.concatenate([up, up], axis=1)
            top[u] = merged
            put_fine(p, e, *act_pair(merged))
        return carry

    lax.fori_loop(0, SLOTS, middle, 0)
    last_down = remote(ha.at[SLOTS], rxa3, 6, right)
    last_up = remote(hb.at[0], rxb3, 7, left)
    last_down.start()
    last_up.start()

    cell_col = iota((C2, C2), 1)
    src = iota((C2, C2), 0)
    weave = jnp.where(cell_col == 2 * (src % C) + src // C, 1.0, 0.0).astype(bf16)

    def decode(i, carry):
        p = (i + 2) % SLOTS

        @pl.when(i == 5)
        def _():
            last_down.wait()
            last_up.wait()
            fine_arrived(rxa3, rxb3)

        for e in range(ENS):
            u = p * ENS + e
            even, odd = act_pair(top[u] + fine_conv(p, e, wdec))
            acts = jnp.concatenate([even, odd], axis=1).astype(bf16)
            mc[2 * e : 2 * e + 2] = acts.reshape(2, MROWS, C2)
        acts = [mc[2 * e : 2 * e + 2].reshape(ROWS, C2) for e in range(ENS)]
        network = jnp.dot(
            jnp.concatenate(acts, axis=1), wout[...], preferred_element_type=f32
        )
        parts = []
        for b in range(4):
            t = network[b * C : (b + 1) * C].T
            t = jnp.concatenate([t[0:16], t[16:32]], axis=1)
            high = t.astype(bf16)
            rest = t - high.astype(f32)
            low = rest.astype(bf16)
            parts += [high, low, (rest - low.astype(f32)).astype(bf16)]
        woven = jnp.dot(jnp.concatenate(parts, axis=0), weave, preferred_element_type=f32)
        blocks = [
            woven[b * 48 : b * 48 + 16] + woven[b * 48 + 16 : b * 48 + 32] + woven[b * 48 + 32 : b * 48 + 48]
            for b in range(4)
        ]
        net = jnp.concatenate(blocks, axis=1)
        state = noisy[p].reshape(16, 1024)
        denoised = c_skip * state + c_out * net
        moved = state + (alive(p) * (STEP_RATIO - 1.0)) * (state - denoised)
        out[p] = moved.reshape(ENS, 4, 1024)
        return carry

    lax.fori_loop(0, SLOTS, decode, 0)


def body(
    noisy, sigma, coarse, row_ids, table_index, interp_table, live_counts, face_len, w_lift,
    noise_embed, kernel_top, w_down, kernel_mid, w_up, kernel_dec, w_out,
):
    vmem = pl.BlockSpec(memory_space=pltpu.VMEM)
    smem = pl.BlockSpec(memory_space=pltpu.SMEM)
    units = SLOTS * ENS
    fine = pltpu.VMEM((units, ROWS, C2), bf16)
    mid = pltpu.VMEM((units, MROWS, C2), bf16)
    face = pltpu.VMEM((SLOTS + 1, ENS, 16, C2), bf16)
    faces = pltpu.VMEM((3, SLOTS + 1, ENS, 16, C2), bf16)
    landed = pltpu.VMEM((ENS, 16, C2), bf16)
    return pl.pallas_call(
        kernel,
        out_shape=jax.ShapeDtypeStruct(noisy.shape, f32),
        in_specs=[
            vmem, smem, vmem, vmem, smem, vmem, smem, smem, vmem, vmem,
            vmem, vmem, vmem, vmem, vmem, vmem,
        ],
        out_specs=vmem,
        scratch_shapes=[
            pltpu.VMEM((16, 2048), bf16),
            pltpu.VMEM((1536, C2), bf16),
            pltpu.VMEM((1536, C2), bf16),
            pltpu.VMEM((2304 + C, C2), bf16),
            pltpu.VMEM((C2, C), bf16),
            pltpu.VMEM((ENS * C2, C), bf16),
            pltpu.VMEM((ENS, C2, C2), bf16),
            pltpu.VMEM((2, ROWS, C2), bf16),
            pltpu.VMEM((units, ROWS, C2), f32),
            fine, fine, face, face, face, face,
            pltpu.VMEM((units, MROWS, C), bf16),
            mid, mid, mid, faces, faces,
            landed, landed, landed, landed, landed, landed,
            pltpu.SemaphoreType.DMA((8,)),
            pltpu.SemaphoreType.DMA((8,)),
        ],
        compiler_params=pltpu.CompilerParams(
            collective_id=0, has_side_effects=True, vmem_limit_bytes=63 * 2**20
        ),
        cost_estimate=pl.CostEstimate(
            flops=45_000_000_000, bytes_accessed=6_000_000, transcendentals=15_000_000
        ),
    )(
        noisy, sigma, coarse, row_ids, table_index, interp_table, live_counts, face_len, w_lift,
        noise_embed.reshape(1, C), kernel_top, w_down, kernel_mid, w_up, kernel_dec, w_out,
    )


def solution(mesh):
    placed = (
        P("patch", None, None, None),
        P(),
        P(None, "patch"),
        P("patch", None),
        P("patch"),
        P(),
        P("patch"),
        P("patch", None),
        P(),
        P(),
        P(),
        P(),
        P(),
        P(),
        P(),
        P(),
    )
    return jax.shard_map(
        body, mesh=mesh, in_specs=placed, out_specs=P("patch", None, None, None), check_vma=False
    )
```

profile of v0, /device:TPU:0, one launch (start us, length us, event | category | flops | bytes accessed | tf_op | source)
XLA Modules:
  0.0 108.3 jit_solution(190944045179123574)
XLA Ops:
  0.7 1.3 %copy.17.face_len = s32[8,2]{1,0:T(8,128)} copy(s32[8,2]{0,1:T(2,128)} %param.23) | data formatting | bytes 128 | tf_op args[7]
  2.0 1.4 %copy.18.w_lift = bf16[128,16]{1,0:T(8,128)(2,1)} copy(bf16[128,16]{0,1:T(8,128)(2,1)} %param.24) | data formatting | bytes 8192 | tf_op args[8]
  3.4 103.0 %shard_map.154 = f32[8,4,4,1024]{3,2,1,0:T(4,128)} custom-call(f32[8,4,4,1024]{3,2,1,0:T(4,128)} %noisy.1, f32[4]{0:T(128)} %sigma.1, bf16[12,1024]{1,0:T(8,128)(2,1)} %coarse.1, s32[8,16]{1,0:T(8,128)} %row_ids.1, s32[8]{0:T(128)} %table_index.1, bf16[8,16,1024]{2,1,0:T(8,128)(2,1)} %interp.1, s32[1]{0:T(128)S(6)} %copy.20.live, s32[8,2]{1,0:T(8,128)} %copy.17.face_len, ...), custom_call_target="tpu_custom_call" | custom-call | flops 44999999488 | bytes 6000000 | tf_op jit(solution)/shard_map/pallas_call | solution.py:403
  106.4 1.9 %copy.21 = f32[8,4,4,1024]{3,2,1,0:T(4,128)} copy(f32[8,4,4,1024]{3,2,1,0:T(4,128)} %shard_map.154) | data formatting | bytes 1048576
where the time goes:
time: 109 us; the launch traced here: 108 us
  Pallas kernels  103 us (94%)
  local copies, waits for them, and re-layouts  4.62 us (4%)
    pallas_call x1, Pallas kernels, body(): pl.pallas_call(kernel, out_shape=jax.ShapeDtypeStruct(noisy.shape, f32),...  103 us
    unnamed x3, local copies, waits for them, and re-layouts  4.62 us

commit v1 on v0

--- a/solution.py
+++ b/solution.py
@@ -28,6 +28,11 @@
     return lax.broadcasted_iota(jnp.int32, shape, dim)
 
 
+def half_rsqrt(x, count):
+    total = jnp.sum(x * x, axis=1, keepdims=True)
+    return lax.rsqrt(total * (4.0 / count) + 4.0 * EPSILON)
+
+
 def half_silu(v, scale):
     h = v * scale
     return h + h * jnp.tanh(h)
@@ -37,26 +42,28 @@
     halves = []
     for k in range(2):
         x = v[:, k * C : (k + 1) * C]
-        scale = 0.5 * lax.rsqrt(jnp.mean(x * x, axis=1, keepdims=True) + EPSILON)
+        scale = half_rsqrt(x, C)
         halves.append(half_silu(x, scale))
     return halves
 
 
 def act_wide(v):
-    scale = 0.5 * lax.rsqrt(jnp.mean(v * v, axis=1, keepdims=True) + EPSILON)
+    scale = half_rsqrt(v, C2)
     return half_silu(v, scale)
 
 
 def from_left(x):
+    x = x.astype(bf16)
     n, c = x.shape
     x3 = x.reshape(n // 16, 16, c)
-    return jnp.where(iota(x3.shape, 1) == 0, 0.0, pltpu.roll(x3, 1, 1)).reshape(n, c)
+    return jnp.where(iota(x3.shape, 1) == 0, jnp.zeros((), bf16), pltpu.roll(x3, 1, 1)).reshape(n, c).astype(bf16)
 
 
 def from_right(x):
+    x = x.astype(bf16)
     n, c = x.shape
     x3 = x.reshape(n // 16, 16, c)
-    return jnp.where(iota(x3.shape, 1) == 15, 0.0, pltpu.roll(x3, 15, 1)).reshape(n, c)
+    return jnp.where(iota(x3.shape, 1) == 15, jnp.zeros((), bf16), pltpu.roll(x3, 15, 1)).reshape(n, c).astype(bf16)
 
 
 def transposed(block):
@@ -68,7 +75,7 @@
     k_top, w_down, k_mid, w_up, k_dec, w_out,
     out,
     cx, wtop, wdec, wmid, wup, wout, wlift, d_in,
-    top, fc, fs, ha, hb, sha, shb, pool, mc, ml, mr, mha, mhb,
+    top, fc, fs, ha, hb, sha, shb, pool, mc, ml, mr, mha, mhb, staged,
     rxa1, rxb1, rxa2, rxb2, rxa3, rxb3, send, recv,
 ):
     n = lax.axis_size("patch")
@@ -84,8 +91,6 @@
     own = jnp.concatenate([coarse[...].astype(f32), jnp.zeros((4, 1024), f32)], axis=0)
     cx[:, 512:1536] = own.astype(bf16)
 
-    pl.semaphore_wait(barrier, 2)
-
     def remote(src, dst, k, device):
         return pltpu.make_async_remote_copy(
             src_ref=src, dst_ref=dst, send_sem=send.at[k], recv_sem=recv.at[k],
@@ -94,9 +99,6 @@
 
     cells_right = remote(cx.at[:, 1024:1536], cx.at[:, 0:512], 0, right)
     cells_left = remote(cx.at[:, 512:1024], cx.at[:, 1536:2048], 1, left)
-    cells_right.start()
-    cells_left.start()
-
     zero = jnp.zeros((C, C), bf16)
     for k_ref, w in ((k_top, wtop), (k_dec, wdec)):
 
@@ -129,22 +131,23 @@
         j = iota((C, 16), 0) % 32
         idx = iota((C, 16), 1)
         pick = ((j // 4 == e) & (idx == j % 4)) | ((j >= 16) & (j < 28) & (idx == j - 12))
-        block = lax.dot_general(
-            jnp.where(pick, 1.0, 0.0).astype(bf16), w_lift[...], NT, preferred_element_type=f32
-        ).astype(bf16)
+        block = jnp.dot(
+            jnp.where(pick, 1.0, 0.0).astype(bf16), w_lift[...], preferred_element_type=f32
+        )
+        b = embed[...] * jnp.log(jnp.full((1, C), sigma[e], f32))
+        for k in range(3):
+            part = b.astype(bf16).astype(f32)
+            block = jnp.where(iota((C, C), 0) % 32 == 28 + k, part, block)
+            b = b - part
+        block = block.astype(bf16)
         wlift[e, 0:C, 0:C] = block
         wlift[e, 0:C, C:C2] = zero
         wlift[e, C:C2, 0:C] = zero
         wlift[e, C:C2, C:C2] = block
 
-    def member(e, f):
-        s = jnp.full((1, C), sigma[e], f32)
-        return f(s)
-
-    bias = []
-    for e in range(ENS):
-        b = embed[...] * member(e, jnp.log)
-        bias.append(jnp.concatenate([b, b], axis=1))
+    pl.semaphore_wait(barrier, 2)
+    cells_right.start()
+    cells_left.start()
 
     def per_row(f):
         r = iota((16, C), 0) // 4
@@ -176,7 +179,8 @@
     picked = jnp.where(pk // 16 == tk // 16, picked, 0.0).astype(bf16)
     stencil = jnp.dot(picked, route, preferred_element_type=f32).astype(bf16)
     tables = interp[...].reshape(C, 1024)
-    cond = jnp.dot(stencil, tables, preferred_element_type=f32).astype(bf16)
+    cond = jnp.dot(stencil, tables, preferred_element_type=f32)
+    cond = jnp.where(iota((C, 1024), 0) % 16 < 12, cond, 1.0).astype(bf16)
     for p in range(SLOTS):
         state = (noisy[p].reshape(16, 1024) * c_in).astype(bf16)
         for b in range(4):
@@ -202,10 +206,10 @@
         return jnp.where(jnp.minimum(p, SLOTS - 1 - p) < live[0], 1.0, 0.0).astype(f32)
 
     def face_of_next(p):
-        return jnp.where(p == SLOTS - 1, 32, face_len[jnp.minimum(p + 1, SLOTS - 1), 0])
+        return jnp.where(p == SLOTS - 1, 32, face_len[0, jnp.minimum(p + 1, SLOTS - 1)])
 
     def face_of_previous(p):
-        return jnp.where(p == 0, 32, face_len[jnp.maximum(p - 1, 0), 1])
+        return jnp.where(p == 0, 32, face_len[1, jnp.maximum(p - 1, 0)])
 
     def put_fine_face(centre, side, slot, e, even, odd, length, keep):
         even = jnp.where(fine_col < length, even, 0.0) * keep
@@ -269,32 +273,45 @@
             a = rxa[e].astype(f32)
             put_fine_face(ha, sha, 0, e, a[:, :C], a[:, C:], face_len[0, 0], has_above)
             b = rxb[e].astype(f32)
-            put_fine_face(hb, shb, SLOTS, e, b[:, :C], b[:, C:], face_len[SLOTS - 1, 1], has_below)
+            put_fine_face(hb, shb, SLOTS, e, b[:, :C], b[:, C:], face_len[1, SLOTS - 1], has_below)
 
     def mid_arrived(rxa, rxb):
         for e in range(ENS):
             put_mid_face(mha, 0, e, rxa[e].astype(f32), face_len[0, 0], has_above)
-            put_mid_face(mhb, SLOTS, e, rxb[e].astype(f32), face_len[SLOTS - 1, 1], has_below)
-
-    def lift(i, carry):
-        p = (i + 2) % SLOTS
+            put_mid_face(mhb, SLOTS, e, rxb[e].astype(f32), face_len[1, SLOTS - 1], has_below)
+
+    def lift(p, e):
         lanes = (iota((1, C2), 1) % C) // 32 == p % 4
         lhs = d_in[p // 4] * jnp.where(lanes, 1.0, 0.0).astype(bf16)
-        for e in range(ENS):
-            hidden = jnp.dot(lhs, wlift[e], preferred_element_type=f32) + bias[e]
-            top[p * ENS + e] = hidden
-            put_fine(p, e, *act_pair(hidden))
+        hidden = jnp.dot(lhs, wlift[e], preferred_element_type=f32)
+        top[p * ENS + e] = hidden
+        put_fine(p, e, *act_pair(hidden))
+
+    def lift_patch(i, carry):
+        for e in range(ENS):
+            lift((i + 5) % SLOTS, e)
         return carry
 
-    lax.fori_loop(0, SLOTS, lift, 0)
+    lax.fori_loop(0, SLOTS - 1, lift_patch, 0)
     face_down = remote(ha.at[SLOTS], rxa1, 2, right)
     face_up = remote(hb.at[0], rxb1, 3, left)
     face_down.start()
     face_up.start()
 
+    def pool_top(p, e):
+        u = p * ENS + e
+        t = top[u] + fine_conv(p, e, wtop)
+        top[u] = t
+        pooled = (t[:, :C] + t[:, C:]).reshape(16, 2, 16, C)
+        pooled = ((pooled[:, 0] + pooled[:, 1]) * 0.25).reshape(MROWS, C).astype(bf16)
+        pool[u] = pooled
+        staged[e, :, 0:C] = pooled
+
+    def project(p, e):
+        d = jnp.dot(staged[e, :, 0:C], wmid[2304:, :], preferred_element_type=f32)
+        put_mid(p, e, act_wide(d))
+
     def encode(i, carry):
-        p = (i + 2) % SLOTS
-
         @pl.when(i == 5)
         def _():
             face_down.wait()
@@ -302,42 +319,46 @@
             fine_arrived(rxa1, rxb1)
 
         for e in range(ENS):
-            u = p * ENS + e
-            t = top[u] + fine_conv(p, e, wtop)
-            top[u] = t
-            pooled = (t[:, :C] + t[:, C:]).reshape(16, 2, 16, C)
-            pooled = ((pooled[:, 0] + pooled[:, 1]) * 0.25).reshape(MROWS, C).astype(bf16)
-            pool[u] = pooled
-            d = jnp.dot(pooled, wmid[2304:, :], preferred_element_type=f32)
-            put_mid(p, e, act_wide(d))
+            project((i + 1) % SLOTS, e)
+            pool_top((i + 2) % SLOTS, e)
         return carry
 
-    lax.fori_loop(0, SLOTS, encode, 0)
+    for e in range(ENS):
+        lift(4, e)
+        pool_top(2, e)
+    lax.fori_loop(1, SLOTS, encode, 0)
     mid_down = remote(mha.at[1, SLOTS], rxa2, 4, right)
     mid_up = remote(mhb.at[1, 0], rxb2, 5, left)
     mid_down.start()
     mid_up.start()
 
+    def mix(p, e):
+        staged[e] = mid_conv(p, e).astype(bf16)
+
+    def merge(p, e):
+        u = p * ENS + e
+        up = jnp.dot(staged[e], wup[...], preferred_element_type=f32).reshape(16, 1, 16, C)
+        up = jnp.broadcast_to(up, (16, 2, 16, C)).reshape(ROWS, C)
+        merged = top[u] + jnp.concatenate([up, up], axis=1)
+        top[u] = merged
+        put_fine(p, e, *act_pair(merged))
+
     def middle(i, carry):
-        p = (i + 2) % SLOTS
-
-        @pl.when(i == 5)
+        @pl.when(i == 4)
         def _():
             mid_down.wait()
             mid_up.wait()
             mid_arrived(rxa2, rxb2)
 
         for e in range(ENS):
-            u = p * ENS + e
-            m = mid_conv(p, e).astype(bf16)
-            up = jnp.dot(m, wup[...], preferred_element_type=f32).reshape(16, 1, 16, C)
-            up = jnp.broadcast_to(up, (16, 2, 16, C)).reshape(ROWS, C)
-            merged = top[u] + jnp.concatenate([up, up], axis=1)
-            top[u] = merged
-            put_fine(p, e, *act_pair(merged))
+            merge((i + 2) % SLOTS, e)
+            mix((i + 3) % SLOTS, e)
         return carry
 
-    lax.fori_loop(0, SLOTS, middle, 0)
+    for e in range(ENS):
+        project(1, e)
+        mix(3, e)
+    lax.fori_loop(1, SLOTS, middle, 0)
     last_down = remote(ha.at[SLOTS], rxa3, 6, right)
     last_up = remote(hb.at[0], rxb3, 7, left)
     last_down.start()
@@ -347,20 +368,12 @@
     src = iota((C2, C2), 0)
     weave = jnp.where(cell_col == 2 * (src % C) + src // C, 1.0, 0.0).astype(bf16)
 
-    def decode(i, carry):
-        p = (i + 2) % SLOTS
-
-        @pl.when(i == 5)
-        def _():
-            last_down.wait()
-            last_up.wait()
-            fine_arrived(rxa3, rxb3)
-
-        for e in range(ENS):
-            u = p * ENS + e
-            even, odd = act_pair(top[u] + fine_conv(p, e, wdec))
-            acts = jnp.concatenate([even, odd], axis=1).astype(bf16)
-            mc[2 * e : 2 * e + 2] = acts.reshape(2, MROWS, C2)
+    def unfold(p, e):
+        even, odd = act_pair(top[p * ENS + e] + fine_conv(p, e, wdec))
+        acts = jnp.concatenate([even, odd], axis=1).astype(bf16)
+        mc[2 * e : 2 * e + 2] = acts.reshape(2, MROWS, C2)
+
+    def finish(p):
         acts = [mc[2 * e : 2 * e + 2].reshape(ROWS, C2) for e in range(ENS)]
         network = jnp.dot(
             jnp.concatenate(acts, axis=1), wout[...], preferred_element_type=f32
@@ -383,9 +396,24 @@
         denoised = c_skip * state + c_out * net
         moved = state + (alive(p) * (STEP_RATIO - 1.0)) * (state - denoised)
         out[p] = moved.reshape(ENS, 4, 1024)
+
+    def decode(i, carry):
+        @pl.when(i == 3)
+        def _():
+            last_down.wait()
+            last_up.wait()
+            fine_arrived(rxa3, rxb3)
+
+        for e in range(ENS):
+            unfold((i + 4) % SLOTS, e)
+        finish((i + 4) % SLOTS)
         return carry
 
-    lax.fori_loop(0, SLOTS, decode, 0)
+    for e in range(ENS):
+        merge(2, e)
+        unfold(4, e)
+    finish(4)
+    lax.fori_loop(1, SLOTS, decode, 0)
 
 
 def body(
@@ -420,7 +448,7 @@
             pltpu.VMEM((units, ROWS, C2), f32),
             fine, fine, face, face, face, face,
             pltpu.VMEM((units, MROWS, C), bf16),
-            mid, mid, mid, faces, faces,
+            mid, mid, mid, faces, faces, pltpu.VMEM((ENS, MROWS, C2), bf16),
             landed, landed, landed, landed, landed, landed,
             pltpu.SemaphoreType.DMA((8,)),
             pltpu.SemaphoreType.DMA((8,)),
@@ -432,7 +460,7 @@
             flops=45_000_000_000, bytes_accessed=6_000_000, transcendentals=15_000_000
         ),
     )(
-        noisy, sigma, coarse, row_ids, table_index, interp_table, live_counts, face_len, w_lift,
+        noisy, sigma, coarse, row_ids, table_index, interp_table, live_counts, face_len.T, w_lift.T,
         noise_embed.reshape(1, C), kernel_top, w_down, kernel_mid, w_up, kernel_dec, w_out,
     )
 

time: 109 us -> 79.7 us (0.73)
  Pallas kernels: 103 us -> 77 us
  local copies, waits for them, and re-layouts: 4.62 us -> 1.87 us
    pallas_call x1, Pallas kernels: 103 us -> 77 us  [body(): pl.pallas_call(kernel, out_shape=jax.ShapeDtypeStruct(noisy.shape, f32),...]
    unnamed x3 -> x1, local copies, waits for them, and re-layouts: 4.62 us -> 1.87 us
where the time goes in v1:
time: 79.7 us; the launch traced here: 79.5 us
  Pallas kernels  77 us (97%)
  local copies, waits for them, and re-layouts  1.87 us (2%)
    pallas_call x1, Pallas kernels, body(): pl.pallas_call(kernel, out_shape=jax.ShapeDtypeStruct(noisy.shape, f32),...  77 us
    unnamed x1, local copies, waits for them, and re-layouts  1.87 us

profile of v1, /device:TPU:0, one launch (start us, length us, event | category | flops | bytes accessed | tf_op | source)
XLA Modules:
  0.0 79.5 jit_solution(3126480483804740467)
XLA Ops:
  0.7 77.0 %shard_map.154 = f32[8,4,4,1024]{3,2,1,0:T(4,128)} custom-call(f32[8,4,4,1024]{3,2,1,0:T(4,128)} %noisy.1, f32[4]{0:T(128)} %sigma.1, bf16[12,1024]{1,0:T(8,128)(2,1)} %coarse.1, s32[8,16]{1,0:T(8,128)} %row_ids.1, s32[8]{0:T(128)} %table_index.1, bf16[8,16,1024]{2,1,0:T(8,128)(2,1)} %interp.1, s32[1]{0:T(128)S(6)} %copy.18.live, s32[2,8]{1,0:T(2,128)} %bitcast.4, ...), custom_call_target="tpu_custom_call" | custom-call | flops 44999999488 | bytes 6000000 | tf_op jit(solution)/shard_map/pallas_call | solution.py:431
  77.7 1.9 %copy.19 = f32[8,4,4,1024]{3,2,1,0:T(4,128)} copy(f32[8,4,4,1024]{3,2,1,0:T(4,128)} %shard_map.154) | data formatting | bytes 1048576

commit v2 on v1

--- a/solution.py
+++ b/solution.py
@@ -53,17 +53,21 @@
 
 
 def from_left(x):
-    x = x.astype(bf16)
     n, c = x.shape
-    x3 = x.reshape(n // 16, 16, c)
-    return jnp.where(iota(x3.shape, 1) == 0, jnp.zeros((), bf16), pltpu.roll(x3, 1, 1)).reshape(n, c).astype(bf16)
+    r = pltpu.roll(x.reshape(n // 8, 8, c), 1, 1).reshape(n // 16, 2, 8, c)
+    edge = iota((n // 16, 8, c), 1) == 0
+    low = jnp.where(edge, 0.0, r[:, 0])
+    high = jnp.where(edge, r[:, 0], r[:, 1])
+    return jnp.stack([low, high], axis=1).reshape(n, c)
 
 
 def from_right(x):
-    x = x.astype(bf16)
     n, c = x.shape
-    x3 = x.reshape(n // 16, 16, c)
-    return jnp.where(iota(x3.shape, 1) == 15, jnp.zeros((), bf16), pltpu.roll(x3, 15, 1)).reshape(n, c).astype(bf16)
+    r = pltpu.roll(x.reshape(n // 8, 8, c), 7, 1).reshape(n // 16, 2, 8, c)
+    edge = iota((n // 16, 8, c), 1) == 7
+    low = jnp.where(edge, r[:, 1], r[:, 0])
+    high = jnp.where(edge, 0.0, r[:, 1])
+    return jnp.stack([low, high], axis=1).reshape(n, c)
 
 
 def transposed(block):
@@ -76,7 +80,7 @@
     out,
     cx, wtop, wdec, wmid, wup, wout, wlift, d_in,
     top, fc, fs, ha, hb, sha, shb, pool, mc, ml, mr, mha, mhb, staged,
-    rxa1, rxb1, rxa2, rxb2, rxa3, rxb3, send, recv,
+    txa, txb, rxa1, rxb1, rxa2, rxb2, rxa3, rxb3, send, recv,
 ):
     n = lax.axis_size("patch")
     me = lax.axis_index("patch")
@@ -112,6 +116,10 @@
             return carry
 
         lax.fori_loop(0, 3, fine_weights, 0)
+
+    pl.semaphore_wait(barrier, 2)
+    cells_right.start()
+    cells_left.start()
 
     def mid_weights(t, carry):
         wmid[pl.ds(pl.multiple_of(t * C2, C2), C2), :] = transposed(k_mid[t])
@@ -145,10 +153,6 @@
         wlift[e, C:C2, 0:C] = zero
         wlift[e, C:C2, C:C2] = block
 
-    pl.semaphore_wait(barrier, 2)
-    cells_right.start()
-    cells_left.start()
-
     def per_row(f):
         r = iota((16, C), 0) // 4
         s = jnp.full((16, C), sigma[0], f32)
@@ -287,16 +291,26 @@
         top[p * ENS + e] = hidden
         put_fine(p, e, *act_pair(hidden))
 
-    def lift_patch(i, carry):
-        for e in range(ENS):
-            lift((i + 5) % SLOTS, e)
-        return carry
-
-    lax.fori_loop(0, SLOTS - 1, lift_patch, 0)
-    face_down = remote(ha.at[SLOTS], rxa1, 2, right)
-    face_up = remote(hb.at[0], rxb1, 3, left)
+    def edge(p, e, at, target):
+        lanes = (iota((1, C2), 1) % C) // 32 == p % 4
+        lhs = d_in[p // 4, at : at + 16] * jnp.where(lanes, 1.0, 0.0).astype(bf16)
+        hidden = jnp.dot(lhs, wlift[e], preferred_element_type=f32)
+        target[e] = jnp.concatenate(act_pair(hidden), axis=1).astype(bf16)
+
+    for e in range(ENS):
+        edge(SLOTS - 1, e, ROWS - 16, txa)
+        edge(0, e, 0, txb)
+    face_down = remote(txa, rxa1, 2, right)
+    face_up = remote(txb, rxb1, 3, left)
     face_down.start()
     face_up.start()
+
+    def lift_patch(p, carry):
+        for e in range(ENS):
+            lift(p, e)
+        return carry
+
+    lax.fori_loop(1, 4, lift_patch, 0)
 
     def pool_top(p, e):
         u = p * ENS + e
@@ -311,13 +325,15 @@
         d = jnp.dot(staged[e, :, 0:C], wmid[2304:, :], preferred_element_type=f32)
         put_mid(p, e, act_wide(d))
 
+    def encode_lift(i, carry):
+        for e in range(ENS):
+            project((i + 1) % SLOTS, e)
+            pool_top((i + 2) % SLOTS, e)
+        for e in range(ENS):
+            lift((i + 4) % SLOTS, e)
+        return carry
+
     def encode(i, carry):
-        @pl.when(i == 5)
-        def _():
-            face_down.wait()
-            face_up.wait()
-            fine_arrived(rxa1, rxb1)
-
         for e in range(ENS):
             project((i + 1) % SLOTS, e)
             pool_top((i + 2) % SLOTS, e)
@@ -326,7 +342,11 @@
     for e in range(ENS):
         lift(4, e)
         pool_top(2, e)
-    lax.fori_loop(1, SLOTS, encode, 0)
+    lax.fori_loop(1, 5, encode_lift, 0)
+    face_down.wait()
+    face_up.wait()
+    fine_arrived(rxa1, rxb1)
+    lax.fori_loop(5, SLOTS, encode, 0)
     mid_down = remote(mha.at[1, SLOTS], rxa2, 4, right)
     mid_up = remote(mhb.at[1, 0], rxb2, 5, left)
     mid_down.start()
@@ -449,7 +469,7 @@
             fine, fine, face, face, face, face,
             pltpu.VMEM((units, MROWS, C), bf16),
             mid, mid, mid, faces, faces, pltpu.VMEM((ENS, MROWS, C2), bf16),
-            landed, landed, landed, landed, landed, landed,
+            landed, landed, landed, landed, landed, landed, landed, landed,
             pltpu.SemaphoreType.DMA((8,)),
             pltpu.SemaphoreType.DMA((8,)),
         ],

time: 79.7 us -> 77.3 us (0.970)
  Pallas kernels: 77 us -> 74.6 us
    pallas_call x1, Pallas kernels: 77 us -> 74.6 us  [body(): pl.pallas_call(kernel, out_shape=jax.ShapeDtypeStruct(noisy.shape, f32),...]
where the time goes in v2:
time: 77.3 us; the launch traced here: 77.1 us
  Pallas kernels  74.6 us (97%)
  local copies, waits for them, and re-layouts  1.87 us (2%)
    pallas_call x1, Pallas kernels, body(): pl.pallas_call(kernel, out_shape=jax.ShapeDtypeStruct(noisy.shape, f32),...  74.6 us
    unnamed x1, local copies, waits for them, and re-layouts  1.87 us

profile of v2, /device:TPU:0, one launch (start us, length us, event | category | flops | bytes accessed | tf_op | source)
XLA Modules:
  0.0 77.1 jit_solution(6203605822480276537)
XLA Ops:
  0.7 74.6 %shard_map.154 = f32[8,4,4,1024]{3,2,1,0:T(4,128)} custom-call(f32[8,4,4,1024]{3,2,1,0:T(4,128)} %noisy.1, f32[4]{0:T(128)} %sigma.1, bf16[12,1024]{1,0:T(8,128)(2,1)} %coarse.1, s32[8,16]{1,0:T(8,128)} %row_ids.1, s32[8]{0:T(128)} %table_index.1, bf16[8,16,1024]{2,1,0:T(8,128)(2,1)} %interp.1, s32[1]{0:T(128)S(6)} %copy.18.live, s32[2,8]{1,0:T(2,128)} %bitcast.4, ...), custom_call_target="tpu_custom_call" | custom-call | flops 44999999488 | bytes 6000000 | tf_op jit(solution)/shard_map/pallas_call | solution.py:451
  75.2 1.9 %copy.19 = f32[8,4,4,1024]{3,2,1,0:T(4,128)} copy(f32[8,4,4,1024]{3,2,1,0:T(4,128)} %shard_map.154) | data formatting | bytes 1048576
